TPU v7x, 32 devices: a whole 2x2x4 slice. The times are simulated.
32 devices in a mesh: dp: 8 (over z, x), tensor: 4 (over y, core).
Axes of the slice: x: 2, y: 2, z: 4, core: 2. Of those that a mesh axis runs over, the one named last changes fastest.
Arguments:
- tokens: bfloat16 [16, 1024, 768], P('dp'), may hold values from -6 to 6
- segments: int32 [16, 1024], P('dp'), may hold values from 0 to 7, never falling along the last dimension, each value on 1 to 512 neighbouring positions
- cotangent: bfloat16 [16, 1024, 768], P('dp'), may hold values from -6 to 6
- block_owner_slots: int32 [4, 48], P('tensor'), may hold values from 0 to 47, as said below
- master_weights: float32 [4, 48, 192, 192], P('tensor', 'dp')
- statistics: float32 [4, 48, 2, 192, 192], P('tensor', 'dp')
- inverse_roots: float32 [4, 48, 2, 192, 192], P('tensor', 'dp')
- shared_vectors: float32 [6, 768], replicated
- shared_state: float32 [6, 768], replicated, may hold values from 1e-07 to 2e-06
- split_bias: float32 [4, 1344], P('tensor'), may hold values from -1.2 to 1.2
- split_state: float32 [4, 1344], P('tensor'), may hold values from 1e-07 to 2e-06
Outputs:
- output: float32 [16, 1024, 768], P('dp')
- input_grad: float32 [16, 1024, 768], P('dp')
- norm: float32 [], replicated
- clipped_grads: float32 [4, 48, 192, 192], P('tensor', 'dp')
- new_master: float32 [4, 48, 192, 192], P('tensor', 'dp')
- master_copy: bfloat16 [4, 48, 192, 192], P('tensor', 'dp')
- new_statistics: float32 [4, 48, 2, 192, 192], P('tensor', 'dp')
- shared_grad: float32 [6, 768], replicated
- shared_new_state: float32 [6, 768], replicated
- shared_new: float32 [6, 768], replicated
- split_grad: float32 [4, 1344], P('tensor')
- split_new_state: float32 [4, 1344], P('tensor')
- split_new: float32 [4, 1344], P('tensor')
Inputs may be any that keep to these rules, and one draw needn't show every extreme that they name: `block_owner_slots`: row t gives each of the 48 blocks of tensor index t a distinct slot; slot s is held by data index s // 6; slots 0 and 47 are used in every row.
All inputs are finite; a program needn't handle non-finite values.
Results may differ from a plain program's by a relative error of at most 0.014.
Values may be sent and summed in bfloat16 or wider, within the bound.
A program may use at most 192 MiB of HBM per device.

v0:
```python
import jax
import jax.numpy as jnp
from jax import lax
from jax.sharding import PartitionSpec as P

HEAD = 64


EPS = 1e-05
NEG = -1000000000.0
DECAY = 0.5
RATE = 0.3
RATE_VECTOR = 0.2
HIGH = lax.Precision.HIGHEST


def layer_norm(value, gain, shift):
    mean = jnp.mean(value, -1, keepdims=True)
    centred = value - mean
    spread = jnp.mean(centred * centred, -1, keepdims=True)
    return centred * lax.rsqrt(spread + EPS) * gain + shift


def gelu_tanh(value):
    return jax.nn.gelu(value, approximate=True)


def to_blocks(matrix, size):
    rows = matrix.shape[0] // size
    cols = matrix.shape[1] // size
    return (
        matrix.reshape(rows, size, cols, size)
        .transpose(0, 2, 1, 3)
        .reshape(rows * cols, size, size)
    )


def from_blocks(blocks, rows, cols):
    size = blocks.shape[-1]
    return (
        blocks.reshape(rows, cols, size, size)
        .transpose(0, 2, 1, 3)
        .reshape(rows * size, cols * size)
    )


def masking(seg):
    places = jnp.arange(seg.shape[0])
    return (seg[:, None] == seg[None, :]) & (places[None, :] <= places[:, None])


def scores_of(query, keys, seg):
    scores = jnp.einsum("qhe,khe->hqk", query, keys, preferred_element_type=jnp.float32) * HEAD ** (
        -0.5
    )
    return jnp.where(masking(seg)[None], scores, NEG)


def attend(items):
    query, keys, values, seg = items
    scores = scores_of(query, keys, seg)
    top = jnp.max(scores, -1, keepdims=True)
    expo = jnp.exp(scores - top)
    total = jnp.sum(expo, -1, keepdims=True)
    probs = (expo / total).astype(jnp.bfloat16)
    mixed = jnp.einsum("hqk,khe->qhe", probs, values, preferred_element_type=jnp.float32)
    return (mixed.astype(jnp.bfloat16), top + jnp.log(total))


def attend_back(items):
    query, keys, values, seg, logsum, d_mixed = items
    scores = scores_of(query, keys, seg)
    probs = jnp.exp(scores - logsum)
    d_probs = jnp.einsum("qhe,khe->hqk", d_mixed, values, preferred_element_type=jnp.float32)
    d_values = jnp.einsum(
        "hqk,qhe->khe", probs.astype(jnp.bfloat16), d_mixed, preferred_element_type=jnp.float32
    )
    centre = jnp.sum(probs * d_probs, -1, keepdims=True)
    d_scores = (probs * (d_probs - centre)).astype(jnp.bfloat16)
    d_query = jnp.einsum(
        "hqk,khe->qhe", d_scores, keys, preferred_element_type=jnp.float32
    ) * HEAD ** (-0.5)
    d_keys = jnp.einsum(
        "hqk,qhe->khe", d_scores, query, preferred_element_type=jnp.float32
    ) * HEAD ** (-0.5)
    return (d_query, d_keys, d_values)


def body(
    tokens,
    segments,
    cotangent,
    block_owner_slots,
    master_weights,
    statistics,
    inverse_roots,
    shared_vectors,
    shared_state,
    split_bias,
    split_state,
):
    size = master_weights.shape[-1]
    slots = master_weights.shape[1]
    lookup_table = block_owner_slots[0]
    every = lax.all_gather(master_weights.astype(jnp.bfloat16), "dp", axis=1, tiled=True)[0]
    blocks = every[lookup_table]
    seqs, length, width = tokens.shape
    rows_grid = width // size
    qkv_cols = 3 * size
    hidden_cols = split_bias.shape[1] - qkv_cols
    fold = hidden_cols // size
    cut_a = 3 * rows_grid
    cut_b = cut_a + rows_grid
    cut_c = cut_b + rows_grid * fold
    w_qkv = from_blocks(blocks[:cut_a], rows_grid, 3)
    w_out = from_blocks(blocks[cut_a:cut_b], 1, rows_grid)
    w_fc = from_blocks(blocks[cut_b:cut_c], rows_grid, fold)
    w_proj = from_blocks(blocks[cut_c:], fold, rows_grid)
    heads = size // HEAD
    count = seqs * length
    gain1, shift1, gain2, shift2 = (
        shared_vectors[0],
        shared_vectors[1],
        shared_vectors[2],
        shared_vectors[3],
    )
    out_bias, proj_bias = (shared_vectors[4], shared_vectors[5])
    qkv_bias = split_bias[0, :qkv_cols]
    fc_bias = split_bias[0, qkv_cols:]
    inputs = tokens.reshape(count, width).astype(jnp.float32)
    h_one = layer_norm(inputs, gain1, shift1).astype(jnp.bfloat16)
    qkv = (jnp.dot(h_one, w_qkv, preferred_element_type=jnp.float32) + qkv_bias).astype(
        jnp.bfloat16
    )
    qkv_heads = qkv.reshape(seqs, length, 3, heads, HEAD)
    query, keys, values = (qkv_heads[:, :, 0], qkv_heads[:, :, 1], qkv_heads[:, :, 2])
    mixed, logsum = lax.map(attend, (query, keys, values, segments))
    mixed_flat = mixed.reshape(count, size)
    attn_part = jnp.dot(mixed_flat, w_out, preferred_element_type=jnp.float32)
    second = inputs + lax.psum(attn_part, "tensor") + out_bias
    h_two = layer_norm(second, gain2, shift2).astype(jnp.bfloat16)
    hidden = jnp.dot(h_two, w_fc, preferred_element_type=jnp.float32) + fc_bias
    gelu_out = gelu_tanh(hidden).astype(jnp.bfloat16)
    branch_part = jnp.dot(gelu_out, w_proj, preferred_element_type=jnp.float32)
    output = (
        second
        + lax.psum(branch_part.astype(jnp.bfloat16), "tensor").astype(jnp.float32)
        + proj_bias
    )
    d_low = cotangent.reshape(count, width)
    d_output = d_low.astype(jnp.float32)
    d_proj_bias = jnp.sum(d_output, 0)
    d_w_proj = jnp.einsum("rf,rd->fd", gelu_out, d_low, preferred_element_type=jnp.float32)
    d_gelu = jnp.einsum("rd,fd->rf", d_low, w_proj, preferred_element_type=jnp.float32)
    gelu_back = jax.vjp(gelu_tanh, hidden)[1]
    d_hidden = gelu_back(d_gelu)[0].astype(jnp.bfloat16)
    d_fc_bias = jnp.sum(d_hidden.astype(jnp.float32), 0)
    d_w_fc = jnp.einsum("rd,rf->df", h_two, d_hidden, preferred_element_type=jnp.float32)
    d_h_part = jnp.einsum("rf,df->rd", d_hidden, w_fc, preferred_element_type=jnp.float32)
    d_h_two = lax.psum(d_h_part, "tensor")
    norm_two_back = jax.vjp(layer_norm, second, gain2, shift2)[1]
    d_second_norm, d_gain2, d_shift2 = norm_two_back(d_h_two)
    d_second = d_output + d_second_norm
    d_second_low = d_second.astype(jnp.bfloat16)
    d_out_bias = jnp.sum(d_second_low.astype(jnp.float32), 0)
    d_w_out = jnp.einsum("rc,rd->cd", mixed_flat, d_second_low, preferred_element_type=jnp.float32)
    d_mixed = jnp.einsum(
        "rd,cd->rc", d_second_low, w_out, preferred_element_type=jnp.float32
    ).astype(jnp.bfloat16)
    d_mixed = d_mixed.reshape(seqs, length, heads, HEAD)
    d_query, d_keys, d_values = lax.map(
        attend_back, (query, keys, values, segments, logsum, d_mixed)
    )
    d_qkv = jnp.stack([d_query, d_keys, d_values], 2).reshape(count, qkv_cols).astype(jnp.bfloat16)
    d_qkv_bias = jnp.sum(d_qkv.astype(jnp.float32), 0)
    d_w_qkv = jnp.einsum("rd,rc->dc", h_one, d_qkv, preferred_element_type=jnp.float32)
    d_one_part = jnp.einsum("rc,dc->rd", d_qkv, w_qkv, preferred_element_type=jnp.float32)
    d_h_one = lax.psum(d_one_part.astype(jnp.bfloat16), "tensor").astype(jnp.float32)
    norm_one_back = jax.vjp(layer_norm, inputs, gain1, shift1)[1]
    d_input_norm, d_gain1, d_shift1 = norm_one_back(d_h_one)
    input_grad = d_second + d_input_norm
    shared_raw = jnp.stack([d_gain1, d_shift1, d_gain2, d_shift2, d_out_bias, d_proj_bias], 0)
    grads = jnp.concatenate(
        [
            to_blocks(d_w_qkv, size),
            to_blocks(d_w_out, size),
            to_blocks(d_w_fc, size),
            to_blocks(d_w_proj, size),
        ],
        0,
    )
    split_raw = jnp.concatenate([d_qkv_bias, d_fc_bias], 0)[None]
    total_slots = lax.axis_size("dp") * slots
    grads, shared_raw, split_raw = lax.psum((grads, shared_raw, split_raw), "dp")
    laid_out = jnp.zeros((total_slots, size, size), jnp.float32).at[lookup_table].set(grads)
    owned = lax.dynamic_slice_in_dim(laid_out, lax.axis_index("dp") * slots, slots, 0)
    first_part = jnp.where(lax.axis_index("tensor") == 0, 1.0, 0.0)
    square = (
        jnp.sum(grads * grads)
        + jnp.sum(split_raw * split_raw)
        + first_part * jnp.sum(shared_raw * shared_raw)
    )
    square = lax.psum(square, "tensor")
    norm = jnp.sqrt(square)
    factor = 1.0 / jnp.maximum(norm, 1.0)
    clipped = owned * factor
    left = DECAY * statistics[0, :, 0] + (1.0 - DECAY) * jnp.einsum(
        "sij,skj->sik", clipped, clipped, precision=HIGH
    )
    right = DECAY * statistics[0, :, 1] + (1.0 - DECAY) * jnp.einsum(
        "sji,sjk->sik", clipped, clipped, precision=HIGH
    )
    step = jnp.einsum("sij,sjk->sik", inverse_roots[0, :, 0], clipped, precision=HIGH)
    step = jnp.einsum("sij,sjk->sik", step, inverse_roots[0, :, 1], precision=HIGH)
    new_master = master_weights[0] - RATE * step
    shared_grad = shared_raw * factor
    shared_new_state = DECAY * shared_state + (1.0 - DECAY) * shared_grad * shared_grad
    shared_new = shared_vectors - RATE_VECTOR * shared_grad * lax.rsqrt(shared_new_state)
    split_grad = split_raw * factor
    split_new_state = DECAY * split_state + (1.0 - DECAY) * split_grad * split_grad
    split_new = split_bias - RATE_VECTOR * split_grad * lax.rsqrt(split_new_state)
    return (
        output.reshape(seqs, length, width),
        input_grad.reshape(seqs, length, width),
        norm,
        clipped[None],
        new_master[None],
        new_master[None].astype(jnp.bfloat16),
        jnp.stack([left, right], 1)[None],
        shared_grad,
        shared_new_state,
        shared_new,
        split_grad,
        split_new_state,
        split_new,
    )


def solution(mesh):
    placed = (
        P("dp", None, None),
        P("dp", None),
        P("dp", None, None),
        P("tensor", None),
        P("tensor", "dp", None, None),
        P("tensor", "dp", None, None, None),
        P("tensor", "dp", None, None, None),
        P(),
        P(),
        P("tensor", None),
        P("tensor", None),
    )
    return jax.shard_map(
        body,
        mesh=mesh,
        in_specs=placed,
        out_specs=(
            P("dp", None, None),
            P("dp", None, None),
            P(),
            P("tensor", "dp", None, None),
            P("tensor", "dp", None, None),
            P("tensor", "dp", None, None),
            P("tensor", "dp", None, None, None),
            P(),
            P(),
            P(),
            P("tensor", None),
            P("tensor", None),
            P("tensor", None),
        ),
        check_vma=False,
    )
```

profile of v0, /device:TPU:0, one launch (start us, length us, event | category | flops | bytes accessed | tf_op | source)
XLA Modules:
  0.0 1029.4 jit_solution(7286871113431467179)
XLA Ops:
  20.3 73.1 %all-gather.2.cloned.1.call-done = bf16[1,48,192,192]{3,2,0,1:T(8,128)(2,1)} async-done(((bf16[1,6,192,192]{3,2,0,1:T(8,128)(2,1)}), bf16[1,48,192,192]{3,2,0,1:T(8,128)(2,1)}) %all-gather.2.cloned.1.call-update) | async-done | bytes 3538960 | tf_op jit(solution)/shard_map/all_gather | solution.py:105
  119.7 40.2 %while.26 = (s32[]{:T(128)}, bf16[2,1024,3,64]{1,3,2,0:T(8,128)(2,1)}, f32[2,3,1024,1]{2,1,3,0:T(4,128)S(1)}, bf16[2,1024,3,64]{1,3,2,0:T(8,128)(2,1)}, s32[2,10...) while((s32[]{:T(128)}, ...), condition=%wide.region_5.6_spmd, body=%wide.region_2.5_spmd.sunk | while | flops 846394368 | bytes 47835264 | solution.py:137
  128.5 5.7 fusion.183
  143.0 5.7 fusion.183
  185.0 100.2 %all-reduce.7.cloned.1.call-done = f32[2048,768]{1,0:T(8,128)} async-done(((f32[2048,768]{1,0:T(8,128)}), f32[2048,768]{1,0:T(8,128)}) %all-reduce.7.cloned.1.call-update) | async-done | bytes 6291472 | tf_op jit(solution)/shard_map/psum | solution.py:140
  292.0 5.8 fusion.74
  297.8 6.9 convert_reduce_fusion.4
  311.5 8.6 convolution_convert_fusion
  320.2 110.8 %all-reduce.9.cloned.1.call-done = f32[2048,768]{1,0:T(8,128)} async-done(((f32[2048,768]{1,0:T(8,128)}), f32[2048,768]{1,0:T(8,128)}) %all-reduce.9.cloned.1.call-update) | async-done | bytes 6291472 | tf_op jit(solution)/shard_map/psum | solution.py:160
  431.0 6.4 multiply_reduce_fusion.2
  450.0 50.7 %while.27 = (s32[]{:T(128)}, bf16[2,1024,3,64]{1,3,2,0:T(8,128)(2,1)}, bf16[2,1024,3,64]{1,3,2,0:T(8,128)(2,1)}, bf16[2,1024,3,64]{1,3,2,0:T(8,128)(2,1)}, bf16[...) while((s32[]{:T(128)}, ...), condition=%wide.region_15.16_spmd, body=%wide.region_13.15_spmd.sunk | while | flops 2063987712 | bytes 116372728 | solution.py:171
  452.7 7.2 multiply_reduce_fusion.8
  459.9 7.0 multiply_convert_fusion.4
  477.9 7.2 multiply_reduce_fusion.8
  485.1 7.0 multiply_convert_fusion.4
  519.9 6.9 fusion.133
  548.5 83.1 %all-reduce.13.cloned.1.call-done = (bf16[2048,768]{1,0:T(8,128)(2,1)}, bf16[2048,768]{1,0:T(8,128)(2,1)}) async-done(((bf16[2048,768]{1,0:T(8,128)(2,1)}, bf16[2048,768]{1,0:T(8,128)(2,1)}), (bf16[2048,768]{1,0:T(8,128)(2,1)}, bf16[2048,768]{1,0:T(8,128)(2,1)})) %all-reduce.13.cloned.1.call-update) | async-done | bytes 6291472 | tf_op jit(solution)/shard_map/psum | solution.py:147
  657.9 39.1 %all-reduce = (f32[1,1344]{1,0:T(1,128)S(1)}, f32[6,768]{1,0:T(8,128)S(1)}) all-reduce(f32[1,1344]{1,0:T(1,128)S(1)} %broadcast_in_dim.99, f32[6,768]{1,0:T(8,128)S(1)} %stack.40), channel_id=1, replica_groups=mesh['dp'=8,'tensor'=4] {'dp'}, use_global_device_ids=true, to_apply=%region_23.24 | all-reduce | flops 5952 | bytes 47616 | tf_op jit(solution)/shard_map/psum | solution.py:194
  698.9 8.9 add_add_fusion.2
  707.8 246.4 %all-reduce.11.cloned.1.call-done = f32[48,192,192]{2,1,0:T(8,128)} async-done(((f32[48,192,192]{2,1,0:T(8,128)}), f32[48,192,192]{2,1,0:T(8,128)}) %all-reduce.11.cloned.1.call-update) | async-done | bytes 7077904 | tf_op jit(solution)/shard_map/psum | solution.py:194
  954.1 6.7 multiply_reduce_fusion.1
  962.2 6.1 add_add_fusion.4
  968.3 7.5 psum.63
  981.2 20.2 %scatter_fusion = f32[48,192,192]{2,1,0:T(8,128)} fusion(f32[48,192,192]{2,1,0:T(8,128)} %broadcast_in_dim.100, s32[48]{0:T(128)S(1)} %copy-done.60, f32[48,192,192]{2,1,0:T(8,128)} %all-reduce.11.cloned.1.call-done), kind=kCustom, calls=%fused_computation.1 | custom fusion | bytes 21233856 | tf_op jit(solution)/shard_map/scatter | solution.py:195
  (267 shorter events, 222.6 us)
Async XLA Ops:
  7.2 9.0 copy-start.1
  7.2 86.2 %all-gather.2.cloned.1.call-start = ((), (), s32[]{:S(2)}) async-start(), calls=%async_computation | async-start | bytes 5308416 | tf_op jit(solution)/shard_map/all_gather | solution.py:105
  9.6 275.7 %all-reduce.7.cloned.1.call-start = ((), (), s32[]{:S(2)}) async-start(), calls=%async_computation.1 | async-start | bytes 12582912 | tf_op jit(solution)/shard_map/psum | solution.py:140
  13.2 7.1 copy-start.36
  13.2 7.1 copy-start.44
  109.6 10.1 copy-start.35
  167.4 263.6 %all-reduce.9.cloned.1.call-start = ((), (), s32[]{:S(2)}) async-start(), calls=%async_computation.2 | async-start | bytes 12582912 | tf_op jit(solution)/shard_map/psum | solution.py:160
  170.9 114.4 %copy-start.2 = (bf16[2,1024,768]{2,1,0:T(8,128)(2,1)S(1)}, bf16[2,1024,768]{2,1,0:T(8,128)(2,1)}, u32[]{:S(2)}) copy-start(bf16[2,1024,768]{2,1,0:T(8,128)(2,1)} %param.15) | copy-start | bytes 9437188
  170.9 114.4 %copy-start.56 = (f32[768]{0:T(1024)S(1)}, f32[768]{0:T(1024)}, u32[]{:S(2)}) copy-start(f32[768]{0:T(1024)} %get-tuple-element.212) | copy-start | bytes 9220
  297.8 6.9 copy-start.63
  311.0 320.6 %all-reduce.13.cloned.1.call-start = ((), (), s32[]{:S(2)}) async-start(), calls=%async_computation.4 | async-start | bytes 12582912 | tf_op jit(solution)/shard_map/psum | solution.py:147
  459.9 7.0 copy-start.31
  485.1 7.0 copy-start.31
  511.5 442.7 %all-reduce.11.cloned.1.call-start = ((), (), s32[]{:S(2)}) async-start(), calls=%async_computation.3 | async-start | bytes 18874368 | tf_op jit(solution)/shard_map/psum | solution.py:194
  539.6 92.0 %copy-start.3 = (bf16[2,1024,768]{2,1,0:T(8,128)(2,1)S(1)}, bf16[2,1024,768]{2,1,0:T(8,128)(2,1)}, u32[]{:S(2)}) copy-start(bf16[2,1024,768]{2,1,0:T(8,128)(2,1)} %param.15) | copy-start | bytes 9437188
  539.6 92.0 %copy-start.37 = (f32[768]{0:T(1024)S(1)}, f32[768]{0:T(1024)}, u32[]{:S(2)}) copy-start(f32[768]{0:T(1024)} %copy-done.36) | copy-start | bytes 9220
  544.5 90.9 %copy-start.47 = (f32[1,8,2,128]{3,2,1,0:T(2,128)S(1)}, f32[1,8,2,128]{3,2,1,0:T(2,128)}, u32[]{:S(2)}) copy-start(f32[1,8,2,128]{3,2,1,0:T(2,128)} %get-tuple-element.279) | copy-start | bytes 24580
  544.5 90.9 %copy-start.45 = (f32[768]{0:T(1024)S(1)}, f32[768]{0:T(1024)}, u32[]{:S(2)}) copy-start(f32[768]{0:T(1024)} %copy-done.44) | copy-start | bytes 9220
  655.1 43.8 %copy-start.42 = (f32[2048]{0:T(1024)S(1)}, f32[2048]{0:T(1024)}, u32[]{:S(2)}) copy-start(f32[2048]{0:T(1024)} %copy-done.41) | copy-start | bytes 24580
  697.0 10.8 %copy-start.38 = (f32[6,768]{1,0:T(8,128)}, f32[6,768]{1,0:T(8,128)S(1)}, u32[]{:S(2)}) copy-start(f32[6,768]{1,0:T(8,128)S(1)} %get-tuple-element.250) | copy-start | bytes 55300
  707.8 254.4 %copy-start.22 = (bf16[2048,768]{1,0:T(8,128)(2,1)S(1)}, bf16[2048,768]{1,0:T(8,128)(2,1)}, u32[]{:S(2)}) copy-start(bf16[2048,768]{1,0:T(8,128)(2,1)} %get-tuple-element.251) | copy-start | bytes 9437188
  707.8 254.4 %copy-start.54 = (f32[768]{0:T(1024)S(1)}, f32[768]{0:T(1024)}, u32[]{:S(2)}) copy-start(f32[768]{0:T(1024)} %get-tuple-element.209) | copy-start | bytes 9220
  968.3 12.9 %copy-start.60 = (s32[48]{0:T(128)S(1)}, s32[48]{0:T(128)}, u32[]{:S(2)}) copy-start(s32[48]{0:T(128)} %copy-done.59) | copy-start | bytes 580
  1003.5 11.5 %copy-start.16 = (f32[1,6,192,192]{3,2,1,0:T(8,128)S(1)}, f32[1,6,192,192]{3,2,1,0:T(8,128)}, u32[]{:S(2)}) copy-start(f32[1,6,192,192]{3,2,1,0:T(8,128)} %param.19) | copy-start | bytes 2654212
  (50 other events, 162.4 us)
Sparse Core Ops, SparseCore 0:
  10.8 82.5 all-gather.1
  167.5 117.7 all-reduce.6
  311.2 119.7 all-reduce.8
  511.6 119.9 all-reduce.12
  655.3 298.8 all-reduce.10
where the time goes:
time: 1040 us; the launch traced here: 1030 us
  waiting for transfers between devices  614 us (59%)
  matrix products  127 us (12%)
  local copies, waits for them, and re-layouts  115 us (11%)
  other arithmetic  96.4 us (9%)
  blocking collectives  46.6 us (4%)
  between operations  18.5 us (2%)
  loops' own time  11.7 us (1%)
    psum x1, waiting for transfers between devices, body(): lax.psum((grads, shared_raw, split_raw), 'dp')  246 us
    psum x1, waiting for transfers between devices, body(): d_h_two = lax.psum(d_h_part, 'tensor')  111 us
    psum x1, waiting for transfers between devices, body(): second = inputs + lax.psum(attn_part, 'tensor') + out_bias  100 us
    psum x1, waiting for transfers between devices, body(): lax.psum(branch_part.astype(jnp.bfloat16), 'tensor').astype(jnp.float32)  83.1 us
    all_gather x1, waiting for transfers between devices, body(): lax.all_gather(master_weights.astype(jnp.bfloat16), 'dp', axis=1, tiled=T...  73.1 us
    psum x1, blocking collectives, body(): lax.psum((grads, shared_raw, split_raw), 'dp')  39.1 us
  transfers between devices with their start and end apart: 5, of which 5 were waited for; matrix products, arithmetic and copies ran while one was open for 8% of the time, Pallas kernels for 0%

commit v1 on v0

v1 whole, which is shorter than its diff:
```python
import functools
import math

import jax
import jax.numpy as jnp
from jax import lax
from jax.sharding import PartitionSpec as P
import jax.experimental.pallas as pl
import jax.experimental.pallas.tpu as pltpu

MESH = pl.DeviceIdType.MESH
PAIR = 2
CORES = 2
LANES = 128
MIB = 2**20


def packed_rows(size):
    return size * size // LANES


def pack_block(block, size):
    half = size // 2
    left = block[:, :LANES]
    right = jnp.concatenate([block[:half, LANES:], block[half:, LANES:]], 1)
    return left, right


def place():
    d = lax.axis_index("dp")
    t = lax.axis_index("tensor")
    return d // PAIR, lax.rem(d, PAIR), t // CORES, lax.rem(t, CORES)


def device(a, b, y, c):
    return (a * PAIR + b, y * CORES + c)


def gather_kernel(line, size, w_ref, out_ref, own, sem_own, s_zr, s_zl, s_x, s_y, s_xy, s_yx, r_z, r_x, r_y, r_xy, r_yx):
    a, b, y, c = place()
    other_b, other_y = 1 - b, 1 - y
    slots = w_ref.shape[0]
    block_rows = packed_rows(size)
    rows = slots * block_rows
    half = rows // 2
    barrier = pltpu.get_barrier_semaphore()
    x_dev = device(a, other_b, y, c)
    y_dev = device(a, b, other_y, c)
    right = device(jnp.minimum(a + 1, line - 1), b, y, c)
    left = device(jnp.maximum(a - 1, 0), b, y, c)
    pl.semaphore_signal(barrier, inc=1, device_id=x_dev, device_id_type=MESH)
    pl.semaphore_signal(barrier, inc=1, device_id=y_dev, device_id_type=MESH)

    @pl.when(a < line - 1)
    def _():
        pl.semaphore_signal(barrier, inc=1, device_id=right, device_id_type=MESH)

    @pl.when(a > 0)
    def _():
        pl.semaphore_signal(barrier, inc=1, device_id=left, device_id_type=MESH)

    def pack(s, carry):
        left_part, right_part = pack_block(w_ref[s].astype(jnp.bfloat16), size)
        start = pl.multiple_of(s * block_rows, 32)
        own[pl.ds(start, size), :] = left_part
        own[pl.ds(pl.multiple_of(start + size, 32), size // 2), :] = right_part
        return carry

    lax.fori_loop(0, slots, pack, 0)
    pl.semaphore_wait(barrier, 2 + jnp.where(a < line - 1, 1, 0) + jnp.where(a > 0, 1, 0))

    def index(at, bb):
        return at * PAIR + bb

    def remote(src, dst, s, r, dev):
        return pltpu.make_async_remote_copy(src_ref=src, dst_ref=dst, send_sem=s, recv_sem=r, device_id=dev, device_id_type=MESH)

    def full(at, s, r, dev, src=None):
        ref = out_ref.at[y, index(at, b)]
        return remote(ref if src is None else src, ref, s, r, dev)

    def part(yy, at, bb, upper, s, r, dev):
        ref = out_ref.at[yy, index(at, bb), pl.ds(0 if upper else half, half)]
        return remote(ref, ref, s, r, dev)

    keep = pltpu.make_async_copy(own, out_ref.at[y, index(a, b)], sem_own)
    keep.start()

    def spread(at, src=None):
        full(at, s_x.at[at], r_x.at[at], x_dev, src).start()
        full(at, s_y.at[at], r_y.at[at], y_dev, src).start()

    def second(at):
        pltpu.make_async_remote_copy(
            src_ref=own, dst_ref=out_ref.at[y, index(at, other_b)], send_sem=s_x.at[at], recv_sem=r_x.at[at], device_id=x_dev, device_id_type=MESH
        ).wait_recv()
        part(y, at, other_b, True, s_yx.at[at], r_yx.at[at], y_dev).start()
        pltpu.make_async_remote_copy(
            src_ref=own, dst_ref=out_ref.at[other_y, index(at, b)], send_sem=s_y.at[at], recv_sem=r_y.at[at], device_id=y_dev, device_id_type=MESH
        ).wait_recv()
        part(other_y, at, b, False, s_xy.at[at], r_xy.at[at], x_dev).start()

    def each(j, do):
        if j == 0:
            do(a)
            return

        @pl.when(a - j >= 0)
        def _():
            do(a - j)

        @pl.when(a + j < line)
        def _():
            do(a + j)

    @pl.when(a < line - 1)
    def _():
        full(a, s_zr.at[a], r_z.at[a], right, own).start()

    @pl.when(a > 0)
    def _():
        full(a, s_zl.at[a], r_z.at[a], left, own).start()

    spread(a, own)
    for j in range(1, line):

        @pl.when(a - j >= 0)
        def _():
            at = a - j
            full(at, s_zr.at[at], r_z.at[at], right).wait_recv()

            @pl.when(a < line - 1)
            def _():
                full(at, s_zr.at[at], r_z.at[at], right).start()

        @pl.when(a + j < line)
        def _():
            at = a + j
            full(at, s_zl.at[at], r_z.at[at], left).wait_recv()

            @pl.when(a > 0)
            def _():
                full(at, s_zl.at[at], r_z.at[at], left).start()

        each(j, spread)
        each(j - 1, second)
    each(line - 1, second)

    def finish(at, carry):
        part(other_y, at, other_b, True, s_yx.at[at], r_yx.at[at], y_dev).wait_recv()
        part(other_y, at, other_b, False, s_xy.at[at], r_xy.at[at], x_dev).wait_recv()
        full(at, s_x.at[at], r_x.at[at], x_dev).wait_send()
        full(at, s_y.at[at], r_y.at[at], y_dev).wait_send()
        part(y, at, other_b, True, s_yx.at[at], r_yx.at[at], y_dev).wait_send()
        part(other_y, at, b, False, s_xy.at[at], r_xy.at[at], x_dev).wait_send()

        @pl.when((at <= a) & (a < line - 1))
        def _():
            full(at, s_zr.at[at], r_z.at[at], right).wait_send()

        @pl.when((at >= a) & (a > 0))
        def _():
            full(at, s_zl.at[at], r_z.at[at], left).wait_send()

        return carry

    lax.fori_loop(0, line, finish, 0)
    keep.wait()


def gather(master, line):
    slots, size, _ = master.shape
    rows = slots * packed_rows(size)
    sems = [pltpu.SemaphoreType.DMA((line,))] * 11
    return pl.pallas_call(
        functools.partial(gather_kernel, line, size),
        out_shape=jax.ShapeDtypeStruct((2, line * PAIR, rows, LANES), jnp.bfloat16),
        in_specs=[pl.BlockSpec(memory_space=pltpu.VMEM)],
        out_specs=pl.BlockSpec(memory_space=pl.ANY),
        scratch_shapes=[pltpu.VMEM((rows, LANES), jnp.bfloat16), pltpu.SemaphoreType.DMA] + sems,
        compiler_params=pltpu.CompilerParams(collective_id=1, has_side_effects=True, vmem_limit_bytes=40 * MIB),
        name="gather",
    )(master)


HEAD = 64
EPS = 1e-05
NEG = -1000000000.0
TOP = 3.0e38
QB = 256
MLP_ROWS = 512
LN_ROWS = 128
F32 = jnp.float32
BF16 = jnp.bfloat16


def dot(a, b):
    return lax.dot_general(a, b, (((1,), (0,)), ((), ())), preferred_element_type=F32)


def dot_nt(a, b):
    return lax.dot_general(a, b, (((1,), (1,)), ((), ())), preferred_element_type=F32)


def dot_tn(a, b):
    return lax.dot_general(a, b, (((0,), (0,)), ((), ())), preferred_element_type=F32)


def centre_of(value):
    mean = jnp.mean(value, -1, keepdims=True)
    centred = value - mean
    spread = jnp.mean(centred * centred, -1, keepdims=True)
    return centred, lax.rsqrt(spread + EPS)


def norm_back(value, d_out, gain):
    centred, scale = centre_of(value)
    hat = centred * scale
    d_hat = d_out * gain
    back = scale * (d_hat - jnp.mean(d_hat, -1, keepdims=True) - hat * jnp.mean(d_hat * hat, -1, keepdims=True))
    return back, hat


def rows_of(start, count):
    return pl.ds(pl.multiple_of(start, count), count)


def column_sum(value):
    return jnp.sum(value, 0, keepdims=True)


def layer_kernel(
    dims,
    table,
    tokens,
    segments,
    cotangent,
    pieces,
    shared,
    split,
    grad_blocks,
    out_pair,
    in_grad,
    vectors,
    x,
    dy,
    held,
    w_qkv,
    w_out,
    w_fc,
    w_proj,
    cap,
    seg_col,
    h_one,
    q_s,
    k_s,
    v_s,
    k_t,
    v_t,
    mixed,
    logsum,
    send_a,
    recv_a,
    send_b,
    recv_b,
    send_c,
    recv_c,
    recv_d,
    second,
    h_two,
    gelu_s,
    d_hid,
    d_mixed,
    d_keys,
    d_vals,
    d_qkv,
    bias_qkv,
    bias_fc,
    sem_in,
    sem_out,
    sa,
    ra,
    sb,
    rb,
    sc,
    rc,
    sd,
    rd,
    so,
    ro,
):
    size, width, count = dims
    a, b, y, c = place()
    partner = device(a, b, y, 1 - c)
    y_dev = device(a, b, 1 - y, c)
    barrier = pltpu.get_barrier_semaphore()
    for dev in (partner, y_dev):
        pl.semaphore_signal(barrier, inc=1, device_id=dev, device_id_type=MESH)

    grid = width // size
    hidden_t = split.shape[1] - 3 * size
    fold = hidden_t // size
    pair = 2 * size
    cut_a, cut_b = 3 * grid, 4 * grid
    cut_c = cut_b + grid * fold
    blocks = cut_c + grid * fold
    heads = pair // HEAD
    hidden = 2 * hidden_t
    steps = count // QB
    block_rows = packed_rows(size)
    half = size // 2

    load_x = pltpu.make_async_copy(tokens.at[y], x, sem_in.at[0])
    load_x.start()
    load_w = pltpu.make_async_copy(pieces, held, sem_in.at[1])
    load_w.start()
    load_dy = pltpu.make_async_copy(cotangent.at[y], dy, sem_in.at[2])
    load_dy.start()

    def remote(src, dst, s, r, dev):
        return pltpu.make_async_remote_copy(src_ref=src, dst_ref=dst, send_sem=s, recv_sem=r, device_id=dev, device_id_type=MESH)

    def swap(send, recv, s, r, at, rows):
        where = pl.ds(at * rows, rows) if isinstance(at, int) else rows_of(at * rows, rows)
        return remote(send.at[where], recv.at[where], s.at[at], r.at[at], partner)

    seg_row = segments[pl.ds(y, 1), :].astype(F32)
    seg_col[...] = jnp.transpose(jnp.broadcast_to(seg_row, (LANES, count)))
    reach = []
    at = 0
    for i in range(steps):
        first = max(0, i - 2) * QB
        wide = (i + 1) * QB - first
        reach.append((first, wide, at))
        key_seg = seg_col[first : first + wide, :]
        key_seg = jnp.concatenate([key_seg] * (QB // LANES), 1)
        key_at = lax.broadcasted_iota(jnp.int32, (wide, QB), 0) + first
        query_at = lax.broadcasted_iota(jnp.int32, (wide, QB), 1) + i * QB
        allowed = (key_seg == seg_row[:, i * QB : (i + 1) * QB]) & (key_at <= query_at)
        cap[at : at + wide, :] = jnp.where(allowed, TOP, NEG)
        at += wide

    bias_qkv[0:1, :] = jnp.concatenate([split[t : t + 1, g * size : (g + 1) * size] for g in range(3) for t in range(2)], 1)
    bias_fc[0:1, :] = jnp.concatenate([split[t : t + 1, 3 * size :] for t in range(2)], 1)
    vectors[...] = jnp.zeros_like(vectors)

    gain1, shift1 = shared[0:1, :], shared[1:2, :]
    gain2, shift2 = shared[2:3, :], shared[3:4, :]
    out_bias, proj_bias = shared[4:5, :], shared[5:6, :]

    load_x.wait()

    def norm_one(i, carry):
        where = rows_of(i * LN_ROWS, LN_ROWS)
        centred, scale = centre_of(x[where, :].astype(F32))
        h_one[where, :] = (centred * scale * gain1 + shift1).astype(BF16)
        return carry

    lax.fori_loop(0, count // LN_ROWS, norm_one, 0)
    load_w.wait()

    def block_at(t, block):
        packed = held[t, table[t, block]]
        tail = packed[size:, :]
        return packed[:size], jnp.concatenate([tail[:, : LANES // 2], tail[:, LANES // 2 :]], 0)

    def put_pair(ref, row, col, first, other):
        left0, right0 = first
        left1, right1 = other
        where = rows_of(row * size, size)
        for k, tile in enumerate(
            (
                left0,
                jnp.concatenate([right0, left1[:, : LANES // 2]], 1),
                jnp.concatenate([left1[:, LANES // 2 :], right1], 1),
            )
        ):
            ref[where, pl.ds(pl.multiple_of(col + k * LANES, LANES), LANES)] = tile

    def build_attention(r, carry):
        for g in range(3):
            put_pair(w_qkv, r, g * pair, block_at(0, r * 3 + g), block_at(1, r * 3 + g))
        return carry

    lax.fori_loop(0, grid, build_attention, 0)

    def build_out(n, carry):
        t, j = n // (grid // 2), lax.rem(n, grid // 2)
        put_pair(w_out, t, j * pair, block_at(t, cut_a + 2 * j), block_at(t, cut_a + 2 * j + 1))
        return carry

    lax.fori_loop(0, 2 * (grid // 2), build_out, 0)

    def build_fc(n, carry):
        t, r = n // grid, lax.rem(n, grid)
        for f in range(0, fold, 2):
            block = cut_b + r * fold + f
            put_pair(w_fc, r, t * hidden_t + f * size, block_at(t, block), block_at(t, block + 1))
        return carry

    lax.fori_loop(0, 2 * grid, build_fc, 0)

    def build_proj(n, carry):
        t, f = n // fold, lax.rem(n, fold)
        for r in range(0, grid, 2):
            block = cut_c + f * grid + r
            put_pair(w_proj, n, r * size, block_at(t, block), block_at(t, block + 1))
        return carry

    lax.fori_loop(0, 2 * fold, build_proj, 0)

    def make_qkv(i, carry):
        where = rows_of(i * QB, QB)
        qkv = dot(h_one[where, :], w_qkv[...]) + bias_qkv[0:1, :]
        q_s[where, :] = (qkv[:, :pair].astype(BF16).astype(F32) * HEAD ** (-0.5)).astype(BF16)
        keys, values = qkv[:, pair : 2 * pair], qkv[:, 2 * pair :]
        k_s[where, :] = keys.astype(BF16)
        v_s[where, :] = values.astype(BF16)
        k_t[:, where] = jnp.transpose(keys).astype(BF16)
        v_t[:, where] = jnp.transpose(values).astype(BF16)
        return carry

    lax.fori_loop(0, steps, make_qkv, 0)
    pl.semaphore_wait(barrier, 2)

    def head_of(value, h):
        lane = lax.broadcasted_iota(jnp.int32, value.shape, 1)
        return jnp.where((lane < HEAD) if h == 0 else (lane >= HEAD), value, jnp.zeros_like(value))

    for i in range(steps):
        first, wide, at = reach[i]
        query_rows = slice(i * QB, (i + 1) * QB)

        def attend(n, carry):
            lanes = pl.ds(pl.multiple_of(n * LANES, LANES), LANES)
            keys = k_s[first : first + wide, lanes]
            query = q_s[query_rows, lanes]
            parts = []
            for h in range(2):
                scores = jnp.minimum(dot_nt(keys, head_of(query, h)), cap[at : at + wide, :])
                top = jnp.max(scores, 0, keepdims=True)
                expo = jnp.exp(scores - top)
                total = jnp.sum(expo, 0, keepdims=True)
                probs = (expo * (1.0 / total)).astype(BF16)
                value_rows = pl.ds(pl.multiple_of(n * LANES + h * HEAD, HEAD), HEAD)
                parts.append(dot(v_t[value_rows, first : first + wide], probs))
                logsum[pl.ds(2 * n + h, 1), query_rows] = top + jnp.log(total)
            mixed[query_rows, lanes] = jnp.transpose(jnp.concatenate(parts, 0)).astype(BF16)
            return carry

        lax.fori_loop(0, heads // 2, attend, 0)
        send_a[query_rows, :] = dot(mixed[query_rows, :], w_out[...]).astype(BF16)
        swap(send_a, recv_a, sa, ra, i, QB).start()

    load_dy.wait()

    fc_cols = pair
    parts_of = hidden // fc_cols
    curve = math.sqrt(2.0 / math.pi)

    def mlp(m, carry):
        for i in range(MLP_ROWS // QB):
            swap(send_a, recv_a, sa, ra, m * (MLP_ROWS // QB) + i, QB).wait_recv()

        def norm_two(i, inner):
            where = rows_of(m * MLP_ROWS + i * LN_ROWS, LN_ROWS)
            total = send_a[where, :].astype(F32) + recv_a[where, :].astype(F32)
            value = x[where, :].astype(F32) + total + out_bias
            second[where, :] = value
            centred, scale = centre_of(value)
            h_two[where, :] = (centred * scale * gain2 + shift2).astype(BF16)
            return inner

        lax.fori_loop(0, MLP_ROWS // LN_ROWS, norm_two, 0)
        where = rows_of(m * MLP_ROWS, MLP_ROWS)

        def strip(n, inner):
            cols = pl.ds(pl.multiple_of(n * fc_cols, LANES), fc_cols)
            hid = dot(h_two[where, :], w_fc[:, cols]) + bias_fc[0:1, cols]
            square = hid * hid
            bend = jnp.tanh(curve * hid * (1.0 + 0.044715 * square))
            up = 0.5 * (1.0 + bend)
            gelu_s[where, cols] = (hid * up).astype(BF16)
            slope = up + 0.5 * hid * (1.0 - bend * bend) * (curve * (1.0 + 3 * 0.044715 * square))
            back = (dot_nt(dy[where, :], w_proj[cols, :]) * slope).astype(BF16)
            d_hid[where, cols] = back
            vectors_fc[0:1, cols] += column_sum(back.astype(F32))
            return inner

        lax.fori_loop(0, parts_of, strip, 0)
        send_b[where, :] = dot(gelu_s[where, :], w_proj[...]).astype(BF16)
        send_c[where, :] = dot_nt(d_hid[where, :], w_fc[...]).astype(BF16)
        swap(send_c, recv_c, sc, rc, m, MLP_ROWS).start()
        swap(send_b, recv_b, sb, rb, m, MLP_ROWS).start()
        return carry

    vectors_fc = bias_fc.at[8:16]
    vectors_fc[...] = jnp.zeros(vectors_fc.shape, F32)
    lax.fori_loop(0, count // MLP_ROWS, mlp, 0)

    def keep_pair(tile, spot0, spot1):
        tile = tile.astype(BF16)
        t0, t1, t2 = (tile[:, k * LANES : (k + 1) * LANES] for k in range(3))
        h = LANES // 2
        for (t, block), left, right in (
            (spot0, t0, t1[:, :h]),
            (spot1, jnp.concatenate([t1[:, h:], t2[:, :h]], 1), t2[:, h:]),
        ):
            held[t, block, :size, :] = left
            held[t, block, size:, :] = jnp.concatenate([right[:half], right[half:]], 1)

    def grad_proj(n, carry):
        got = dot_tn(gelu_s[:, pl.ds(pl.multiple_of(n * pair, LANES), pair)], dy[...])
        for s in range(2):
            t, f = (2 * n + s) // fold, lax.rem(2 * n + s, fold)
            for r in range(0, grid, 2):
                block = cut_c + f * grid + r
                keep_pair(got[s * size : (s + 1) * size, r * size : (r + 2) * size], (t, block), (t, block + 1))
        return carry

    lax.fori_loop(0, hidden // pair, grad_proj, 0)

    def grad_fc(n, carry):
        t, m = n // (width // pair), lax.rem(n, width // pair)
        got = dot_tn(h_two[:, pl.ds(pl.multiple_of(m * pair, LANES), pair)], d_hid[:, pl.ds(pl.multiple_of(t * hidden_t, LANES), hidden_t)])
        for s in range(2):
            for f in range(0, fold, 2):
                block = cut_b + (2 * m + s) * fold + f
                keep_pair(got[s * size : (s + 1) * size, f * size : (f + 2) * size], (t, block), (t, block + 1))
        return carry

    lax.fori_loop(0, 2 * (width // pair), grad_fc, 0)

    def store(first, last, sem):
        return pltpu.make_async_copy(held.at[:, pl.ds(first, last - first)], grad_blocks.at[:, pl.ds(first, last - first)], sem)

    store(cut_b, blocks, sem_out.at[0]).start()

    for m in range(count // MLP_ROWS):
        swap(send_b, recv_b, sb, rb, m, MLP_ROWS).wait_recv()
        swap(send_c, recv_c, sc, rc, m, MLP_ROWS).wait_recv()

    def norm_two_back(i, carry):
        d_gain, d_shift, d_bias, d_proj = carry
        where = rows_of(i * LN_ROWS, LN_ROWS)
        value = second[where, :]
        total = send_b[where, :].astype(F32) + recv_b[where, :].astype(F32)
        recv_b[where, :] = (value + total + proj_bias).astype(BF16)
        d_norm = send_c[where, :].astype(F32) + recv_c[where, :].astype(F32)
        d_out = dy[where, :].astype(F32)
        back, hat = norm_back(value, d_norm, gain2)
        d_second = d_out + back
        second[where, :] = d_second
        low = d_second.astype(BF16)
        recv_c[where, :] = low
        return (
            d_gain + column_sum(d_norm * hat),
            d_shift + column_sum(d_norm),
            d_bias + column_sum(low.astype(F32)),
            d_proj + column_sum(d_out),
        )

    zero = jnp.zeros((1, width), F32)
    sums = lax.fori_loop(0, count // LN_ROWS, norm_two_back, (zero,) * 4)
    for k, row in enumerate(sums):
        vectors[2 + k : 3 + k, :width] = row
    d_low = recv_c

    own_half = rows_of(c * (count // 2), count // 2)
    other_half = rows_of((1 - c) * (count // 2), count // 2)
    keep_out = pltpu.make_async_copy(recv_b, out_pair.at[y], sem_out.at[1])
    keep_out.start()
    cross = remote(recv_b.at[own_half], out_pair.at[y, own_half], so.at[0], ro.at[0], y_dev)
    cross.start()

    d_vals[...] = jnp.zeros_like(d_vals)
    d_keys[...] = jnp.zeros_like(d_keys)

    def make_d_mixed(i, carry):
        where = rows_of(i * QB, QB)
        d_mixed[where, :] = dot_nt(d_low[where, :], w_out[...]).astype(BF16)
        return carry

    lax.fori_loop(0, steps, make_d_mixed, 0)

    got = dot_tn(mixed[...], d_low[...])
    for t in range(2):
        for r in range(0, grid, 2):
            keep_pair(got[t * size : (t + 1) * size, r * size : (r + 2) * size], (t, cut_a + r), (t, cut_a + r + 1))

    for i in range(steps):
        first, wide, at = reach[i]
        query_rows = slice(i * QB, (i + 1) * QB)

        def attend_back(n, carry):
            lanes = pl.ds(pl.multiple_of(n * LANES, LANES), LANES)
            key_rows = slice(first, first + wide)
            keys = k_s[key_rows, lanes]
            values = v_s[key_rows, lanes]
            query = q_s[query_rows, lanes]
            d_out = d_mixed[query_rows, lanes]
            d_query = []
            d_value_sum = d_vals[key_rows, lanes]
            d_key_sum = d_keys[key_rows, lanes]
            for h in range(2):
                query_h, d_out_h = head_of(query, h), head_of(d_out, h)
                scores = jnp.minimum(dot_nt(keys, query_h), cap[at : at + wide, :])
                probs = jnp.exp(scores - logsum[pl.ds(2 * n + h, 1), query_rows])
                d_probs = dot_nt(values, d_out_h)
                centre = jnp.sum(probs * d_probs, 0, keepdims=True)
                d_scores = (probs * (d_probs - centre)).astype(BF16)
                d_value_sum += dot(probs.astype(BF16), d_out_h)
                d_key_sum += dot(d_scores, query_h)
                value_rows = pl.ds(pl.multiple_of(n * LANES + h * HEAD, HEAD), HEAD)
                d_query.append(dot(k_t[value_rows, key_rows], d_scores))
            d_vals[key_rows, lanes] = d_value_sum
            d_keys[key_rows, lanes] = d_key_sum
            d_qkv[query_rows, lanes] = (jnp.transpose(jnp.concatenate(d_query, 0)) * HEAD ** (-0.5)).astype(BF16)
            return carry

        lax.fori_loop(0, heads // 2, attend_back, 0)

    cross.wait_recv()
    forward = remote(out_pair.at[1 - y, own_half], out_pair.at[1 - y, own_half], so.at[1], ro.at[1], partner)
    forward.start()
    for i in range(steps):
        swap(send_a, recv_a, sa, ra, i, QB).wait_send()

    def make_d_one(i, carry):
        where = rows_of(i * QB, QB)
        d_qkv[where, pair : 2 * pair] = d_keys[where, :].astype(BF16)
        d_qkv[where, 2 * pair :] = d_vals[where, :].astype(BF16)
        send_a[where, :] = dot_nt(d_qkv[where, :], w_qkv[...]).astype(BF16)
        swap(send_a, recv_d, sd, rd, i, QB).start()
        return carry + column_sum(d_qkv[where, :].astype(F32))

    d_bias_qkv = lax.fori_loop(0, steps, make_d_one, jnp.zeros((1, 3 * pair), F32))
    for t in range(2):
        vectors[6 + t : 7 + t, : 3 * size] = jnp.concatenate(
            [d_bias_qkv[:, (2 * g + t) * size : (2 * g + t + 1) * size] for g in range(3)], 1
        )
        vectors[6 + t : 7 + t, 3 * size : 3 * size + hidden_t] = vectors_fc[0:1, t * hidden_t : (t + 1) * hidden_t]

    def grad_qkv(n, carry):
        m, g = n // 3, lax.rem(n, 3)
        got = dot_tn(h_one[:, pl.ds(pl.multiple_of(m * pair, LANES), pair)], d_qkv[:, pl.ds(pl.multiple_of(g * pair, LANES), pair)])
        for s in range(2):
            block = (2 * m + s) * 3 + g
            keep_pair(got[s * size : (s + 1) * size, :], (0, block), (1, block))
        return carry

    lax.fori_loop(0, 3 * (width // pair), grad_qkv, 0)
    if grad_blocks.shape[1] > blocks:
        held[:, blocks] = jnp.zeros(held.shape[:1] + held.shape[2:], BF16)
        store(blocks, blocks + 1, sem_out.at[3]).start()
    store(0, cut_b, sem_out.at[2]).start()

    def norm_one_back(i, carry):
        d_gain, d_shift = carry
        where = rows_of(i * LN_ROWS, LN_ROWS)
        d_norm = send_a[where, :].astype(F32) + recv_d[where, :].astype(F32)
        back, hat = norm_back(x[where, :].astype(F32), d_norm, gain1)
        in_grad[where, :] = (second[where, :] + back).astype(BF16)
        return d_gain + column_sum(d_norm * hat), d_shift + column_sum(d_norm)

    for i in range(steps):
        swap(send_a, recv_d, sd, rd, i, QB).wait_recv()
    sums = lax.fori_loop(0, count // LN_ROWS, norm_one_back, (zero,) * 2)
    for k, row in enumerate(sums):
        vectors[k : k + 1, :width] = row

    for m in range(count // MLP_ROWS):
        swap(send_b, recv_b, sb, rb, m, MLP_ROWS).wait_send()
        swap(send_c, recv_c, sc, rc, m, MLP_ROWS).wait_send()
    for i in range(steps):
        swap(send_a, recv_d, sd, rd, i, QB).wait_send()
    store(cut_b, blocks, sem_out.at[0]).wait()
    store(0, cut_b, sem_out.at[2]).wait()
    if grad_blocks.shape[1] > blocks:
        store(blocks, blocks + 1, sem_out.at[3]).wait()
    keep_out.wait()
    cross.wait_send()
    forward.wait_send()
    remote(out_pair.at[1 - y, other_half], out_pair.at[1 - y, other_half], so.at[1], ro.at[1], partner).wait_recv()


def layer(table, tokens, segments, cotangent, pieces, shared, split, collective_id=2):
    seqs, count, width = tokens.shape
    _, slots, block_rows, _ = pieces.shape
    size = int(round(math.sqrt(block_rows * LANES)))
    pair = 2 * size
    hidden = 2 * (split.shape[1] - 3 * size)
    blocks = table.shape[1]
    steps = count // QB
    halves = count // MLP_ROWS
    spans = sum((i + 1 - max(0, i - 2)) * QB for i in range(steps))
    wide_vec = -(-split.shape[1] // LANES) * LANES
    vm = lambda shape, kind=BF16: pltpu.VMEM(shape, kind)
    dma = lambda n: pltpu.SemaphoreType.DMA((n,))
    anywhere = pl.BlockSpec(memory_space=pl.ANY)
    inside = pl.BlockSpec(memory_space=pltpu.VMEM)
    act = (count, width)
    return pl.pallas_call(
        functools.partial(layer_kernel, (size, width, count)),
        out_shape=(
            jax.ShapeDtypeStruct((2, min(blocks + 1, slots), block_rows, LANES), BF16),
            jax.ShapeDtypeStruct((2, count, width), BF16),
            jax.ShapeDtypeStruct((count, width), BF16),
            jax.ShapeDtypeStruct((8, wide_vec), F32),
        ),
        in_specs=[pl.BlockSpec(memory_space=pltpu.SMEM), anywhere, inside, anywhere, anywhere, inside, inside],
        out_specs=(anywhere, anywhere, inside, inside),
        scratch_shapes=[
            vm(act),
            vm(act),
            vm((2, slots, block_rows, LANES)),
            vm((width, 3 * pair)),
            vm((pair, width)),
            vm((width, hidden)),
            vm((hidden, width)),
            vm((spans, QB), F32),
            vm((count, LANES), F32),
            vm(act),
            vm((count, pair)),
            vm((count, pair)),
            vm((count, pair)),
            vm((pair, count)),
            vm((pair, count)),
            vm((count, pair)),
            vm((8, count), F32),
            vm(act),
            vm(act),
            vm(act),
            vm(act),
            vm(act),
            vm(act),
            vm(act),
            vm(act, F32),
            vm(act),
            vm((count, hidden)),
            vm((count, hidden)),
            vm((count, pair)),
            vm((count, pair), F32),
            vm((count, pair), F32),
            vm((count, 3 * pair)),
            vm((8, 3 * pair), F32),
            vm((16, hidden), F32),
            dma(3),
            dma(4),
            dma(steps),
            dma(steps),
            dma(halves),
            dma(halves),
            dma(halves),
            dma(halves),
            dma(steps),
            dma(steps),
            dma(2),
            dma(2),
        ],
        compiler_params=pltpu.CompilerParams(collective_id=collective_id, has_side_effects=True, vmem_limit_bytes=63 * MIB),
        name="layer",
    )(table, tokens, segments, cotangent, pieces, shared, split)


SHARE = 0.72
ROW_TILE = 32


def hand_on(line, at):
    turn = lambda dest: dest + line - at if dest < at else line - dest + at
    return sorted(range(line), key=lambda dest: line if dest == at else turn(dest))


def scatter_kernel(
    dims,
    where_from,
    blocks,
    vec,
    d_in,
    total_ref,
    vec_out,
    square_out,
    d_in_other,
    stage,
    from_x_u,
    from_x_l,
    from_y_l,
    from_y_u,
    from_z,
    vec_plane,
    vec_line,
    sq_plane,
    sq_line,
    s_xu,
    r_xu,
    s_xl,
    r_xl,
    s_yl,
    r_yl,
    s_yu,
    r_yu,
    s_z,
    r_z,
    s_v,
    r_v,
    s_vz,
    r_vz,
    s_q,
    r_q,
    s_qz,
    r_qz,
    s_in,
    r_in,
):
    line, slots, upper, chips = dims
    a, b, y, c = place()
    ob, oy, oc = 1 - b, 1 - y, 1 - c
    block_rows = blocks.shape[2]
    rows = slots * block_rows
    lower = rows - upper
    count = d_in.shape[0]
    x_dev, y_dev, core_dev = device(a, ob, y, c), device(a, b, oy, c), device(a, b, y, oc)
    right = device(jnp.minimum(a + 1, line - 1), b, y, c)
    left = device(jnp.maximum(a - 1, 0), b, y, c)
    up, low = pl.ds(0, upper), pl.ds(upper, lower)

    plane = []
    for k in range(1, 8):
        fb, fy, fc = (b + k // 4) % 2, (y + (k // 2) % 2) % 2, (c + k % 2) % 2
        plane.append((k, device(a, fb, fy, fc)))
    planes = [(k, lax.rem(a + k, line)) for k in range(1, line)]
    barrier = pltpu.get_barrier_semaphore()
    for _, dev in plane:
        pl.semaphore_signal(barrier, inc=1, device_id=dev, device_id_type=MESH)
    for _, at in planes:
        pl.semaphore_signal(barrier, inc=1, device_id=device(at, b, y, c), device_id_type=MESH)

    def remote(src, dst, s, r, dev):
        return pltpu.make_async_remote_copy(src_ref=src, dst_ref=dst, send_sem=s, recv_sem=r, device_id=dev, device_id_type=MESH)

    def dest(k):
        return sum(jnp.where(a == p, hand_on(line, p)[k], 0) for p in range(line))

    def fill(at):
        def one(n, carry):
            t, bb, j = n // (PAIR * slots), lax.rem(n // slots, PAIR), lax.rem(n, slots)
            block = blocks[t, where_from[t, (at * PAIR + bb) * slots + j]]
            stage[t, at, bb, pl.ds(pl.multiple_of(j * block_rows, ROW_TILE), block_rows), :] = block
            return carry

        lax.fori_loop(0, 2 * PAIR * slots, one, 0)

    def copy_xu(at):
        return remote(stage.at[:, at, ob, up], from_x_u.at[at], s_xu.at[at], r_xu.at[at], x_dev)

    def copy_yl(at):
        return remote(stage.at[oy, at, :, low], from_y_l.at[at], s_yl.at[at], r_yl.at[at], y_dev)

    def copy_yu(at):
        return remote(stage.at[oy, at, b, up], from_y_u.at[at], s_yu.at[at], r_yu.at[at], y_dev)

    def copy_xl(at):
        return remote(stage.at[y, at, ob, low], from_x_l.at[at], s_xl.at[at], r_xl.at[at], x_dev)

    def copy_z(at, side, dev):
        return remote(stage.at[y, at, b], from_z.at[side, at], s_z.at[at], r_z.at[side, at], dev)

    def add(t, at, bb, first, size, other):
        step = 288 if size % 288 == 0 else 16

        def one(n, carry):
            start = pl.multiple_of(n * step, 16)
            mine = pl.ds(first + start, step)
            stage[t, at, bb, mine, :] = (
                stage[t, at, bb, mine, :].astype(F32) + other[pl.ds(start, step), :].astype(F32)
            ).astype(BF16)
            return carry

        lax.fori_loop(0, size // step, one, 0)

    def copy_in(k):
        part = pl.ds(pl.multiple_of(c * (count // 2) + k * (count // 2 // line), 16), count // 2 // line)
        return remote(d_in.at[part], d_in_other.at[part], s_in.at[k], r_in.at[k], y_dev)

    def first(k):
        at = dest(k)
        fill(at)
        copy_xu(at).start()
        copy_yl(at).start()
        copy_in(k).start()

    def second(k):
        at = dest(k)
        copy_xu(at).wait_recv()
        for t in range(2):
            add(t, at, b, 0, upper, from_x_u.at[at, t])
        copy_yu(at).start()
        copy_yl(at).wait_recv()
        for bb in range(PAIR):
            add(y, at, bb, upper, lower, from_y_l.at[at, bb])
        copy_xl(at).start()

    def third(k):
        at = dest(k)
        copy_yu(at).wait_recv()
        add(y, at, b, 0, upper, from_y_u.at[at])
        copy_xl(at).wait_recv()
        add(y, at, b, upper, lower, from_x_l.at[at])

    def pass_on(turn):
        down = turn - line + a

        @pl.when((down >= 0) & (down < a))
        def _():
            @pl.when(a < line - 1)
            def _():
                copy_z(down, 1, left).wait_recv()
                add(y, down, b, 0, rows, from_z.at[1, down])

            copy_z(down, 1, left).start()

        upw = line - turn + a

        @pl.when((upw > a) & (upw < line))
        def _():
            @pl.when(a > 0)
            def _():
                copy_z(upw, 0, right).wait_recv()
                add(y, upw, b, 0, rows, from_z.at[0, upw])

            copy_z(upw, 0, right).start()

    same_core = [(k, dev) for k, dev in plane if k % 2 == 0]

    def vec_copy(k, dev):
        return remote(vec, vec_plane.at[b * 2 + y], s_v.at[k], r_v.at[b * 2 + y], dev)

    def vec_copy_z(k, at):
        return remote(vec_out, vec_line.at[a], s_vz.at[k], r_vz.at[a], device(at, b, y, c))

    pl.semaphore_wait(barrier, 7 + line - 1)
    for k, dev in same_core:
        vec_copy(k, dev).start()
    vec_plane[b * 2 + y] = vec[...]

    for step in range(line + 2):
        if step < line:
            first(step)
        if step == 1 or line == 1:
            for k, _ in same_core:
                slot = ((b + k // 4) % 2) * 2 + (y + (k // 2) % 2) % 2
                remote(vec, vec_plane.at[slot], s_v.at[k], r_v.at[slot], x_dev).wait()
            vec_out[...] = vec_plane[0] + vec_plane[1] + vec_plane[2] + vec_plane[3]
            for k, at in planes:
                vec_copy_z(k, at).start()
            vec_line[a] = vec_out[...]
        if 0 <= step - 1 < line:
            second(step - 1)
        if 0 <= step - 2 < line:
            third(step - 2)
            if step - 1 < line:
                pass_on(step - 1)

    for k, at in planes:
        remote(vec_out, vec_line.at[at], s_vz.at[k], r_vz.at[at], x_dev).wait()
    vec_sum = vec_line[0]
    for p in range(1, line):
        vec_sum = vec_sum + vec_line[p]
    vec_out[...] = vec_sum

    @pl.when(a > 0)
    def _():
        copy_z(a, 0, right).wait_recv()

    @pl.when(a < line - 1)
    def _():
        copy_z(a, 1, left).wait_recv()

    def finish(n, carry):
        part = pl.ds(pl.multiple_of(n * block_rows, ROW_TILE), block_rows)
        value = stage[y, a, b, part, :].astype(F32)
        value += jnp.where(a > 0, from_z[0, a, part, :].astype(F32), 0.0)
        value += jnp.where(a < line - 1, from_z[1, a, part, :].astype(F32), 0.0)
        total_ref[part, :] = value
        return carry + jnp.sum((value * value).reshape(block_rows // 8, 8, LANES), 0)

    square = lax.fori_loop(0, slots, finish, jnp.zeros((8, LANES), F32))
    row = lax.broadcasted_iota(jnp.int32, (8, LANES), 0)
    weight = jnp.where(row < 6, 1.0 / (chips * CORES), 1.0 / chips)
    for k in range(vec_sum.shape[1] // LANES):
        piece = vec_sum[:, k * LANES : (k + 1) * LANES]
        square += weight * piece * piece
    square_out[...] = square

    def sq_copy(k, dev, slot):
        return remote(square_out, sq_plane.at[slot], s_q.at[k], r_q.at[slot], dev)

    me = b * 4 + y * 2 + c
    for k, dev in plane:
        sq_copy(k, dev, me).start()
    sq_plane[me] = square

    half = pl.ds(pl.multiple_of(c * (count // 2), 16), count // 2)
    for k in range(line):
        copy_in(k).wait_recv()
    share = remote(d_in_other.at[half], d_in_other.at[half], s_in.at[line], r_in.at[line], core_dev)
    share.start()

    for k, dev in plane:
        fb, fy, fc = (b + k // 4) % 2, (y + (k // 2) % 2) % 2, (c + k % 2) % 2
        sq_copy(k, dev, fb * 4 + fy * 2 + fc).wait()
    square = sq_plane[0]
    for k in range(1, 8):
        square = square + sq_plane[k]
    square_out[...] = square
    for k, at in planes:
        remote(square_out, sq_line.at[a], s_qz.at[k], r_qz.at[a], device(at, b, y, c)).start()
    sq_line[a] = square

    share.wait()
    for k in range(line):
        copy_in(k).wait_send()

    def sent(at, carry):
        copy_xu(at).wait_send()
        copy_yl(at).wait_send()
        copy_yu(at).wait_send()
        copy_xl(at).wait_send()

        @pl.when(at != a)
        def _():
            copy_z(at, 0, right).wait_send()

        return carry

    lax.fori_loop(0, line, sent, 0)
    for k, at in planes:
        remote(square_out, sq_line.at[at], s_qz.at[k], r_qz.at[at], x_dev).wait()
    square = sq_line[0]
    for p in range(1, line):
        square = square + sq_line[p]
    square_out[...] = square


def scatter(where_from, blocks, vec, d_in, line, slots):
    block_rows = blocks.shape[2]
    rows = slots * block_rows
    upper = int(rows * SHARE) // 16 * 16
    if slots % 2 == 0 and rows % 576 == 0:
        upper = int(rows * SHARE) // 288 * 288
    lower = rows - upper
    vm = lambda shape, kind=BF16: pltpu.VMEM(shape, kind)
    dma = lambda *n: pltpu.SemaphoreType.DMA(n)
    anywhere = pl.BlockSpec(memory_space=pl.ANY)
    inside = pl.BlockSpec(memory_space=pltpu.VMEM)
    chips = line * PAIR * 2
    return pl.pallas_call(
        functools.partial(scatter_kernel, (line, slots, upper, chips)),
        out_shape=(
            jax.ShapeDtypeStruct((rows, LANES), F32),
            jax.ShapeDtypeStruct(vec.shape, F32),
            jax.ShapeDtypeStruct((8, LANES), F32),
            jax.ShapeDtypeStruct(d_in.shape, BF16),
        ),
        in_specs=[pl.BlockSpec(memory_space=pltpu.SMEM), inside, inside, anywhere],
        out_specs=(inside, inside, inside, anywhere),
        scratch_shapes=[
            vm((2, line, PAIR, rows, LANES)),
            vm((line, 2, upper, LANES)),
            vm((line, lower, LANES)),
            vm((line, PAIR, lower, LANES)),
            vm((line, upper, LANES)),
            vm((2, line, rows, LANES)),
            vm((4,) + vec.shape, F32),
            vm((line,) + vec.shape, F32),
            vm((8, 8, LANES), F32),
            vm((line, 8, LANES), F32),
        ]
        + [dma(line)] * 8
        + [dma(line), dma(2, line)]
        + [dma(8), dma(4), dma(line), dma(line), dma(8), dma(8), dma(line), dma(line), dma(line + 1), dma(line + 1)],
        compiler_params=pltpu.CompilerParams(collective_id=3, has_side_effects=True, vmem_limit_bytes=56 * MIB),
        name="scatter",
    )(where_from, blocks, vec, d_in)


DECAY = 0.5
RATE = 0.3
RATE_VECTOR = 0.2
HIGH = lax.Precision.HIGHEST


def exact(a, b, dims):
    return lax.dot_general(a, b, (dims, ((), ())), precision=HIGH, preferred_element_type=F32)


def update_kernel(
    grad, square, vec, master, stats, roots, shared, shared_state, split, split_state,
    norm_out, clipped_out, master_out, copy_out, stats_out, shared_grad, shared_new_state, shared_new,
    split_grad, split_new_state, split_new,
):
    size = master.shape[-1]
    y = lax.axis_index("tensor") // CORES
    norm = jnp.sqrt(jnp.sum(square[...], keepdims=True))
    factor = 1.0 / jnp.maximum(norm, 1.0)
    packed = grad[0] * factor
    tail = packed[size:]
    h = LANES // 2
    clipped = jnp.concatenate([packed[:size], jnp.concatenate([tail[:, :h], tail[:, h:]], 0)], 1)
    clipped_out[0, 0] = clipped
    stats_out[0, 0, 0] = DECAY * stats[0, 0, 0] + (1.0 - DECAY) * exact(clipped, clipped, ((1,), (1,)))
    stats_out[0, 0, 1] = DECAY * stats[0, 0, 1] + (1.0 - DECAY) * exact(clipped, clipped, ((0,), (0,)))
    step = exact(exact(roots[0, 0, 0], clipped, ((1,), (0,))), roots[0, 0, 1], ((1,), (0,)))
    new = master[0, 0] - RATE * step
    master_out[0, 0] = new
    copy_out[0, 0] = new.astype(BF16)

    @pl.when(pl.program_id(0) == 0)
    def _():
        norm_out[...] = norm
        for raw, value, state, g_out, s_out, v_out in (
            (vec[0 : shared.shape[0], : shared.shape[1]], shared, shared_state, shared_grad, shared_new_state, shared_new),
            (vec[pl.ds(6 + y, 1), :][:, : split.shape[1]], split, split_state, split_grad, split_new_state, split_new),
        ):
            g = raw * factor
            moment = DECAY * state[...] + (1.0 - DECAY) * g * g
            g_out[...] = g
            s_out[...] = moment
            v_out[...] = value[...] - RATE_VECTOR * g * lax.rsqrt(moment)


def update(grad, square, vec, master, stats, roots, shared, shared_state, split, split_state):
    _, slots, size, _ = master.shape
    grad = grad.reshape(slots, -1, LANES)
    whole = lambda shape: pl.BlockSpec(shape, lambda i: (0,) * len(shape))
    one = lambda shape: pl.BlockSpec(shape, lambda i: (0, i) + (0,) * (len(shape) - 2))
    blk, two = one((1, 1, size, size)), one((1, 1, 2, size, size))
    S = jax.ShapeDtypeStruct
    vec_spec, split_spec = whole(shared.shape), whole(split.shape)
    return pl.pallas_call(
        update_kernel,
        grid=(slots,),
        out_shape=(
            S((1, 1), F32), S(master.shape, F32), S(master.shape, F32), S(master.shape, BF16), S(stats.shape, F32),
        ) + (S(shared.shape, F32),) * 3 + (S(split.shape, F32),) * 3,
        in_specs=[pl.BlockSpec((1,) + grad.shape[1:], lambda i: (i, 0, 0)), whole(square.shape), whole(vec.shape), blk, two, two,
                  vec_spec, vec_spec, split_spec, split_spec],
        out_specs=(whole((1, 1)), blk, blk, blk, two) + (vec_spec,) * 3 + (split_spec,) * 3,
        compiler_params=pltpu.CompilerParams(vmem_limit_bytes=32 * MIB),
        name="update",
    )(grad, square, vec, master, stats, roots, shared, shared_state, split, split_state)


def body(
    tokens,
    segments,
    cotangent,
    block_owner_slots,
    master_weights,
    statistics,
    inverse_roots,
    shared_vectors,
    shared_state,
    split_bias,
    split_state,
):
    _, slots, size, _ = master_weights.shape
    ranks = lax.axis_size("dp")
    line = ranks // PAIR
    blocks = block_owner_slots.shape[1]
    y = lax.axis_index("tensor") // CORES
    swap = [(t, (t + CORES) % (2 * CORES)) for t in range(2 * CORES)]

    def both(value):
        other = lax.ppermute(value, "tensor", swap)
        return jnp.where(y == 0, jnp.concatenate([value, other]), jnp.concatenate([other, value]))

    table = both(block_owner_slots)
    split = both(split_bias)
    number = jnp.arange(blocks, dtype=jnp.int32)
    hit = table[:, :, None] == jnp.arange(ranks * slots, dtype=jnp.int32)[None, None]
    where_from = jnp.sum(jnp.where(hit, number[None, :, None] - blocks, 0), 1) + blocks

    pieces = gather(master_weights[0], line)
    pieces = pieces.reshape(2, ranks * slots, packed_rows(size), LANES)
    grad_blocks, out_pair, d_in, vec = layer(table, tokens, segments, cotangent, pieces, shared_vectors, split)
    grad, vec, square, d_in_other = scatter(where_from, grad_blocks, vec, d_in, line, slots)
    updated = update(
        grad, square, vec, master_weights, statistics, inverse_roots, shared_vectors, shared_state, split_bias, split_state
    )
    output = out_pair.astype(F32)
    input_grad = jnp.where(y == 0, jnp.stack([d_in, d_in_other]), jnp.stack([d_in_other, d_in])).astype(F32)
    return (output, input_grad, updated[0].reshape(())) + tuple(updated[1:])


def solution(mesh):
    placed = (
        P("dp", None, None),
        P("dp", None),
        P("dp", None, None),
        P("tensor", None),
        P("tensor", "dp", None, None),
        P("tensor", "dp", None, None, None),
        P("tensor", "dp", None, None, None),
        P(),
        P(),
        P("tensor", None),
        P("tensor", None),
    )
    return jax.shard_map(
        body,
        mesh=mesh,
        in_specs=placed,
        out_specs=(
            P("dp", None, None),
            P("dp", None, None),
            P(),
            P("tensor", "dp", None, None),
            P("tensor", "dp", None, None),
            P("tensor", "dp", None, None),
            P("tensor", "dp", None, None, None),
            P(),
            P(),
            P(),
            P("tensor", None),
            P("tensor", None),
            P("tensor", None),
        ),
        check_vma=False,
    )
```

time: 1040 us -> 268 us (0.26)
  waiting for transfers between devices: 614 us -> 0.01 us
  Pallas kernels: 0 us -> 247 us
  matrix products: 127 us -> 0 us
  local copies, waits for them, and re-layouts: 115 us -> 4.8 us
  other arithmetic: 96.4 us -> 11.6 us
  blocking collectives: 46.6 us -> 0 us
  between operations: 18.5 us -> 0.95 us
  loops' own time: 11.7 us -> 0 us
    psum x4 -> x0, waiting for transfers between devices: 541 us -> none  [the longest x1 246 us: body(): lax.psum((grads, shared_raw, split_raw), 'dp')]
    pallas_call x0 -> x4, Pallas kernels: none -> 247 us  [the longest x1 91.3 us: scatter(): pl.pallas_call(functools.partial(scatter_kernel, (line, slots, upper, chi...]
    dot_general x30 -> x0, matrix products: 127 us -> none  [the longest x2 14.3 us: attend_back(): jnp.einsum('qhe,khe->hqk', d_mixed, values, preferred_element_type=jnp.fl...]
    all_gather x1 -> x0, waiting for transfers between devices: 73.1 us -> none  [body(): lax.all_gather(master_weights.astype(jnp.bfloat16), 'dp', axis=1, tiled=T...]
    reduce_sum x16 -> x1, other arithmetic: 50.9 us -> 0.1 us  [body(): jnp.sum(jnp.where(hit, number[None, :, None] - blocks, 0), 1) + blocks]
    psum x2 -> x0, blocking collectives: 46.6 us -> none  [the longest x1 39.1 us: body(): lax.psum((grads, shared_raw, split_raw), 'dp')]
    reshape x15 -> x0, local copies, waits for them, and re-layouts: 30.7 us -> none  [the longest x4 9.47 us: from_blocks(): return blocks.reshape(rows, cols, size, size).transpose(0, 2, 1, 3).resha...]
    scatter x1 -> x0, local copies, waits for them, and re-layouts: 20.2 us -> none  [body(): jnp.zeros((total_slots, size, size), jnp.float32).at[lookup_table]]
  transfers between devices with their start and end apart: 5 -> 2, of which waited for: 5 -> 0; matrix products, arithmetic and copies ran while one was open for 8% -> 0% of each run, Pallas kernels for 0% -> 23%
where the time goes in v1:
time: 268 us; the launch traced here: 267 us
  Pallas kernels  247 us (92%)
  other arithmetic  11.6 us (4%)
  local copies, waits for them, and re-layouts  4.8 us (2%)
  starting transfers between devices  3.11 us (1%)
    pallas_call x1, Pallas kernels, scatter(): pl.pallas_call(functools.partial(scatter_kernel, (line, slots, upper, chi...  91.3 us
    pallas_call x1, Pallas kernels, layer(): pl.pallas_call(functools.partial(layer_kernel, (size, width, count)), out...  84.8 us
    pallas_call x1, Pallas kernels, gather(): pl.pallas_call(functools.partial(gather_kernel, line, size), out_shape=ja...  61.7 us
    pallas_call x1, Pallas kernels, update(): pl.pallas_call(update_kernel, grid=(slots,), out_shape=(S((1, 1), F32), S...  9.29 us
  transfers between devices with their start and end apart: 2, of which 0 were waited for; matrix products, arithmetic and copies ran while one was open for 0% of the time, Pallas kernels for 23%

profile of v1, /device:TPU:0, one launch (start us, length us, event | category | flops | bytes accessed | tf_op | source)
XLA Modules:
  0.0 267.4 jit_solution(14563053918208456618)
XLA Ops:
  0.6 3.0 %collective-permute-start = (s32[1,48]{1,0:T(1,128)}, s32[1,48]{1,0:T(1,128)S(1)}, u32[]{:S(2)}, u32[]{:S(2)}) collective-permute-start(s32[1,48]{1,0:T(1,128)} %param.14), channel_id=1, source_target_pairs={{0,2},{1,3},{2,0},{3,1},{4,6},{5,7},{6,4},{7,5},{8,10},{9,11},{10,... | collective-permute-start | bytes 584 | tf_op jit(solution)/shard_map/ppermute | solution.py:1176
  3.7 0.1 collective-permute-start.1
  3.8 1.3 copy-done.1
  5.0 61.7 %gather.1 = bf16[2,8,1728,128]{3,2,1,0:T(8,128)(2,1)S(1)} custom-call(f32[6,192,192]{2,1,0:T(8,128)S(1)} %bitcast.7), custom_call_target="tpu_custom_call" | custom-call | tf_op jit(solution)/shard_map/gather/pallas_call | solution.py:175
  66.7 0.0 copy-start
  66.7 2.9 %copy-done = bf16[2,8,1728,128]{3,2,1,0:T(8,128)(2,1)} copy-done((bf16[2,8,1728,128]{3,2,1,0:T(8,128)(2,1)}, bf16[2,8,1728,128]{3,2,1,0:T(8,128)(2,1)S(1)}, u32[]{:S(2)}) %copy-start) | copy-done | bytes 7077912
  69.7 0.0 collective-permute-done
  69.7 0.0 copy-start.13
  69.7 0.1 select_reduce_fusion
  69.8 0.6 broadcast_add_fusion.where_from
  70.4 0.0 collective-permute-done.1
  70.4 0.6 maximum_select_fusion.1.split
  71.0 84.8 %layer.1 = (bf16[2,48,288,128]{3,2,1,0:T(8,128)(2,1)}, bf16[2,1024,768]{2,1,0:T(8,128)(2,1)}, bf16[1024,768]{1,0:T(8,128)(2,1)}, f32[8,1408]{1,0:T(8,128)}) custom-call(s32[2,48]{1,0:T(2,128)} %copy-done.13, bf16[2,1024,768]{2,1,0:T(8,128)(2,1)} %tokens.1, s32[2,1024]{1,0:T(2,128)} %segments.1, bf16[2,1024,768]{2,1,0:T(8,128)(2,1)} %cotangent.1, ...), custom_call_target="tpu_custom_call" | custom-call | tf_op jit(solution)/shard_map/layer/pallas_call | solution.py:703
  155.8 5.1 %convert_element_type.6 = f32[2,1024,768]{2,1,0:T(8,128)} convert(bf16[2,1024,768]{2,1,0:T(8,128)(2,1)} %get-tuple-element.32) | non-fusion elementwise | flops 1572864 | bytes 9437184 | tf_op jit(solution)/shard_map/convert_element_type | solution.py:1192
  160.9 91.3 %scatter.1 = (f32[1728,128]{1,0:T(8,128)}, f32[8,1408]{1,0:T(8,128)}, f32[8,128]{1,0:T(8,128)}, bf16[1024,768]{1,0:T(8,128)(2,1)}) custom-call(s32[2,48]{1,0:T(2,128)} %broadcast_add_fusion.where_from, bf16[2,48,288,128]{3,2,1,0:T(8,128)(2,1)} %get-tuple-element.34.blocks, f32[8,1408]{1,0:T(8,128)} %get-tuple-element.35.vec, ...), custom_call_target="tpu_custom_call" | custom-call | tf_op jit(solution)/shard_map/scatter/pallas_call | solution.py:1058
  252.2 0.0 copy-start.2
  252.2 0.0 copy-start.3
  252.2 0.0 copy-start.4
  252.2 0.0 copy-start.6
  252.2 0.0 copy-start.8
  252.2 0.0 copy-start.10
  252.3 5.2 %fusion = f32[2,1024,768]{2,1,0:T(8,128)} fusion(bf16[1,1024,768]{2,1,0:T(8,128)(2,1)} %bitcast.10, bf16[1,1024,768]{2,1,0:T(8,128)(2,1)S(1)} %bitcast.9, pred[]{:T(512)S(6)} %eq.8), kind=kLoop, calls=%fused_computation.1 | loop fusion | flops 6291456 | bytes 9437185 | tf_op jit(solution)/shard_map/convert_element_type | solution.py:1193
  257.4 0.5 copy-done.5
  258.0 9.3 %update.1 = (f32[1,1]{1,0:T(1,128)}, f32[1,6,192,192]{3,2,1,0:T(8,128)}, f32[1,6,192,192]{3,2,1,0:T(8,128)}, bf16[1,6,192,192]{3,2,1,0:T(8,128)(2,1)}, f32[1,6,2...) custom-call(f32[6,288,128]{2,1,0:T(8,128)S(1)} %bitcast.8, ...), custom_call_target="tpu_custom_call" | custom-call | tf_op jit(solution)/shard_map/update/pallas_call | solution.py:1141
  (21 shorter events, 0.1 us)
Async XLA Ops:
  0.6 69.0 %collective-permute-start = (s32[1,48]{1,0:T(1,128)}, s32[1,48]{1,0:T(1,128)S(1)}, u32[]{:S(2)}, u32[]{:S(2)}) collective-permute-start(s32[1,48]{1,0:T(1,128)} %param.14), channel_id=1, source_target_pairs={{0,2},{1,3},{2,0},{3,1},{4,6},{5,7},{6,4},{7,5},{8,10},{9,11},{10,... | collective-permute-start | bytes 584 | tf_op jit(solution)/shard_map/ppermute | solution.py:1176
  3.7 66.7 %collective-permute-start.1 = (f32[1,1344]{1,0:T(1,128)}, f32[1,1344]{1,0:T(1,128)S(1)}, u32[]{:S(2)}, u32[]{:S(2)}) collective-permute-start(f32[1,1344]{1,0:T(1,128)} %split.1), channel_id=1, source_target_pairs={{0,2},{1,3},{2,0},{3,1},{4,6},{5,7},{6,4},{7,5},{8,10},{9,11},{10,... | collective-permute-start | bytes 16136 | tf_op jit(solution)/shard_map/ppermute | solution.py:1176
  3.8 1.3 copy-start.1
  5.0 64.6 %copy-start.14 = (s32[1,48]{1,0:T(1,128)S(1)}, s32[1,48]{1,0:T(1,128)}, u32[]{:S(2)}) copy-start(s32[1,48]{1,0:T(1,128)} %param.14) | copy-start | bytes 580
  5.0 65.3 %copy-start.9 = (f32[1,1344]{1,0:T(1,128)S(1)}, f32[1,1344]{1,0:T(1,128)}, u32[]{:S(2)}) copy-start(f32[1,1344]{1,0:T(1,128)} %split.1) | copy-start | bytes 16132
  66.7 2.9 %copy-start = (bf16[2,8,1728,128]{3,2,1,0:T(8,128)(2,1)}, bf16[2,8,1728,128]{3,2,1,0:T(8,128)(2,1)S(1)}, u32[]{:S(2)}) copy-start(bf16[2,8,1728,128]{3,2,1,0:T(8,128)(2,1)S(1)} %gather.1) | copy-start | bytes 21233668
  69.7 1.3 copy-start.13
  160.9 91.3 %copy-start.12 = (bf16[1024,768]{1,0:T(8,128)(2,1)S(1)}, bf16[1024,768]{1,0:T(8,128)(2,1)}, u32[]{:S(2)}) copy-start(bf16[1024,768]{1,0:T(8,128)(2,1)} %get-tuple-element.33.d_in) | copy-start | bytes 4718596
  252.2 5.3 %copy-start.2 = (f32[1,6,192,192]{3,2,1,0:T(8,128)S(1)}, f32[1,6,192,192]{3,2,1,0:T(8,128)}, u32[]{:S(2)}) copy-start(f32[1,6,192,192]{3,2,1,0:T(8,128)} %master.1) | copy-start | bytes 2654212
  252.2 5.3 %copy-start.3 = (f32[1,6,2,192,192]{4,3,2,1,0:T(8,128)S(1)}, f32[1,6,2,192,192]{4,3,2,1,0:T(8,128)}, u32[]{:S(2)}) copy-start(f32[1,6,2,192,192]{4,3,2,1,0:T(8,128)} %stats.1) | copy-start | bytes 5308420
  252.2 5.3 %copy-start.4 = (f32[1,6,2,192,192]{4,3,2,1,0:T(8,128)S(1)}, f32[1,6,2,192,192]{4,3,2,1,0:T(8,128)}, u32[]{:S(2)}) copy-start(f32[1,6,2,192,192]{4,3,2,1,0:T(8,128)} %roots.1) | copy-start | bytes 5308420
  252.2 5.8 %copy-start.5 = (f32[1728,128]{1,0:T(8,128)S(1)}, f32[1728,128]{1,0:T(8,128)}, u32[]{:S(2)}) copy-start(f32[1728,128]{1,0:T(8,128)} %get-tuple-element.37) | copy-start | bytes 2654212
  252.2 5.8 %copy-start.6 = (f32[6,768]{1,0:T(8,128)S(1)}, f32[6,768]{1,0:T(8,128)}, u32[]{:S(2)}) copy-start(f32[6,768]{1,0:T(8,128)} %shared.3) | copy-start | bytes 55300
  252.2 5.8 %copy-start.7 = (f32[8,1408]{1,0:T(8,128)S(1)}, f32[8,1408]{1,0:T(8,128)}, u32[]{:S(2)}) copy-start(f32[8,1408]{1,0:T(8,128)} %get-tuple-element.39.vec) | copy-start | bytes 135172
  252.2 5.8 %copy-start.8 = (f32[6,768]{1,0:T(8,128)S(1)}, f32[6,768]{1,0:T(8,128)}, u32[]{:S(2)}) copy-start(f32[6,768]{1,0:T(8,128)} %shared_state.1) | copy-start | bytes 55300
  252.2 5.7 %copy-start.10 = (f32[1,1344]{1,0:T(1,128)S(1)}, f32[1,1344]{1,0:T(1,128)}, u32[]{:S(2)}) copy-start(f32[1,1344]{1,0:T(1,128)} %split_state.1) | copy-start | bytes 16132
  252.2 5.7 %copy-start.11 = (f32[8,128]{1,0:T(8,128)S(1)}, f32[8,128]{1,0:T(8,128)}, u32[]{:S(2)}) copy-start(f32[8,128]{1,0:T(8,128)} %get-tuple-element.38.square) | copy-start | bytes 12292
